TPU v7x, 256 devices: a whole 4x4x8 slice. The times are simulated.
256 devices in a mesh: row: 32 (over x_hi, z, core), col: 8 (over y, x_lo).
Axes of the slice: x: 4 (x_hi: 2, x_lo: 2; x = x_hi * 2 + x_lo), y: 4, z: 8, core: 2. Of those that a mesh axis runs over, the one named last changes fastest.
Arguments:
- eigenvectors: float32 [65536, 4096], P('row', 'col'), may hold values from -6 to 6
- band_v0: float32 [65536, 128], P('row'), may hold values from -0.45 to 1, as said below
- band_w0: float32 [65536, 128], P('row'), may hold values from -0.15625 to 0.15625
- band_v1: float32 [65536, 128], P('row'), may hold values from -0.45 to 1, as said below
- band_w1: float32 [65536, 128], P('row'), may hold values from -0.15625 to 0.15625
- panel_y: float32 [65536, 128], P(('row', 'col')), may hold values from -0.0234375 to 0.0234375
- panel_w: float32 [65536, 128], P(('row', 'col')), may hold values from -0.25 to 0.25
Outputs:
- rotated: float32 [65536, 4096], P('row', 'col')
Inputs may be any that keep to these rules, and one draw needn't show every extreme that they name: In each aligned group of 256 rows, column c of band_v0 is one at the group's row c, may be nonzero at its rows c + 1 to c + 127, and is zero elsewhere. `band_v1`: as band_v0, with groups that begin 128 rows before the aligned ones (the first one cut off at row 0).
All inputs are finite; a program needn't handle non-finite values.
Results may differ from a plain program's by a relative error of at most 0.000076.
Values sent between devices are 32-bit elements; how exact they have to be, the bound alone decides.
A program may use at most 128 MiB of HBM per device.

v0:
```python
import jax
import jax.numpy as jnp
from jax import lax
from jax.sharding import PartitionSpec as P

highest = lax.Precision.HIGHEST


def with_halo(shard, sides, width):
    for axis, dim in sides:
        size, length = (lax.axis_size(axis), shard.shape[dim])
        up = [(i, (i + 1) % size) for i in range(size - 1)]
        down = [(j, i) for i, j in up]
        last = lax.slice_in_dim(shard, length - width, length, axis=dim)
        first = lax.slice_in_dim(shard, 0, width, axis=dim)
        before = lax.ppermute(last, axis, up)
        after = lax.ppermute(first, axis, down)
        shard = jnp.concatenate([before, shard, after], axis=dim)
    return shard


def grouped(matrix, vectors, weights, height):
    groups = matrix.shape[0] // height
    blocks = matrix.reshape(groups, height, matrix.shape[1])
    vec_blocks = vectors.reshape(groups, height, vectors.shape[1])
    wt_blocks = weights.reshape(groups, height, weights.shape[1])
    projected = jnp.einsum("gik,gic->gkc", vec_blocks, blocks, precision=highest)
    update = jnp.einsum("gik,gkc->gic", wt_blocks, projected, precision=highest)
    return (blocks - update).reshape(matrix.shape)


def local(eigenvectors, band_v0, band_w0, band_v1, band_w1, panel_y, panel_w):
    band_width = band_v0.shape[1]
    local_rows = eigenvectors.shape[0]
    columns = eigenvectors.shape[1]
    after_one = grouped(eigenvectors, band_v0, band_w0, 2 * band_width)
    packed = jnp.concatenate([after_one, band_v1, band_w1], 1)
    extended = with_halo(packed, (("row", 0),), band_width)
    after_two = grouped(
        extended[:, :columns],
        extended[:, columns : columns + band_width],
        extended[:, columns + band_width :],
        2 * band_width,
    )[band_width : band_width + local_rows]
    rows_y, rows_w = (
        lax.all_gather(panel_y, "col", axis=0, tiled=True),
        lax.all_gather(panel_w, "col", axis=0, tiled=True),
    )
    partial_value = jnp.einsum("ik,ic->kc", rows_y, after_two, precision=highest)
    summed = lax.psum(partial_value, "row")
    return after_two - jnp.dot(
        rows_w, summed, precision=highest, preferred_element_type=jnp.float32
    )


def solution(mesh):
    placed = (
        P("row", "col"),
        P("row", None),
        P("row", None),
        P("row", None),
        P("row", None),
        P(("row", "col"), None),
        P(("row", "col"), None),
    )
    return jax.shard_map(
        local, mesh=mesh, in_specs=placed, out_specs=P("row", "col"), check_vma=False
    )
```

profile of v0, /device:TPU:1, one launch (start us, length us, event | category | flops | bytes accessed | tf_op | source)
XLA Modules:
  0.0 387.9 jit_solution(8353346630751521428)
XLA Ops:
  6.5 0.0 copy-start
  6.5 0.0 all-gather.3.cloned.1.call-start
  6.5 0.7 all-gather.3.cloned.1.call-update
  7.3 0.0 all-gather.5.cloned.1.call-start
  7.3 0.0 copy-start.3
  7.3 5.3 %fusion.1 = f32[8,128,512]{2,1,0:T(8,128)S(1)} fusion(f32[8,256,128]{2,1,0:T(8,128)} %bitcast.37, f32[8,256,512]{2,1,0:T(8,128)} %bitcast.33), kind=kOutput, calls=%fused_computation.11 | convolution fusion | flops 1610612736 | bytes 7340032 | tf_op jit(solution)/shard_map/gik,gic->gkc/dot_general | solution.py:27
  12.6 0.0 copy-done
  12.6 0.0 copy-done.3
  12.6 0.0 copy-start.4
  12.6 0.0 copy-start.5
  12.6 3.5 bitcast_subtract_fusion.1
  16.2 0.0 copy-start.1
  16.2 2.0 copy-done.1
  18.2 0.0 copy-done.4
  18.2 0.0 copy-done.5
  18.2 1.0 pad_maximum_fusion.5
  19.2 4.9 %collective-permute-start = (f32[128,768]{1,0:T(8,128)}, f32[128,768]{1,0:T(8,128)S(1)}, u32[]{:S(2)}, u32[]{:S(2)}) collective-permute-start(f32[128,768]{1,0:T(8,128)} %get-tuple-element.7), channel_id=1, source_target_pairs={{0,8},{8,16},{16,24},{24,32},{32,40},{40,48},{48,56},{56,64},{64,7... | collective-permute-start | bytes 1179656 | tf_op jit(solution)/shard_map/ppermute | solution.py:16
  24.1 1.9 collective-permute-start.1
  26.0 0.0 all-gather.5.cloned.1.call-update
  26.0 0.2 all-reduce.2.cloned.1.call-start
  26.3 2.8 collective-permute-done
  29.1 4.7 %collective-permute-done.1 = f32[128,768]{1,0:T(8,128)} collective-permute-done((f32[128,768]{1,0:T(8,128)}, f32[128,768]{1,0:T(8,128)}, u32[]{:S(2)}, u32[]{:S(2)}) %collective-permute-start.1) | collective-permute-done | bytes 393248 | tf_op jit(solution)/shard_map/ppermute | solution.py:17
  33.8 3.6 pad_maximum_fusion
  37.4 0.0 copy-start.2
  37.4 0.7 slice.24
  38.1 1.5 copy-done.2
  39.6 1.0 pad_maximum_fusion.1
  40.6 3.1 fusion.2
  43.8 5.6 %convolution_subtract_fusion = f32[9,256,512]{2,1,0:T(8,128)} fusion(f32[9,256,512]{2,1,0:T(8,128)S(1)} %bitcast.30, f32[9,256,128]{2,1,0:T(8,128)S(1)} %bitcast.35, f32[9,128,512]{2,1,0:T(8,128)S(1)} %fusion.2), kind=kOutput, calls=%fused_computation.3 | convolution fusion | flops 1813118976 | bytes 12976128 | tf_op jit(solution)/shard_map/gik,gkc->gic/dot_general | solution.py:28
  49.4 5.5 %all-gather.3.cloned.1.call-done = f32[2048,128]{1,0:T(8,128)} async-done(((f32[256,128]{1,0:T(8,128)}), f32[2048,128]{1,0:T(8,128)}) %all-gather.3.cloned.1.call-update) | async-done | bytes 1048592 | tf_op jit(solution)/shard_map/all_gather | solution.py:46
  54.9 9.9 %convolution_bitcast_fusion = f32[128,512]{0,1:T(8,128)} fusion(f32[2048,128]{1,0:T(8,128)} %all-gather.3.cloned.1.call-done, f32[2304,512]{1,0:T(8,128)} %bitcast.31), kind=kOutput, calls=%fused_computation.6 | convolution fusion | flops 1610612736 | bytes 5505024 | tf_op jit(solution)/shard_map/ik,ic->kc/dot_general | solution.py:49
  64.7 0.0 all-reduce.2.cloned.1.call-update
  64.8 4.6 %slice.25 = f32[2048,512]{1,0:T(8,128)} slice(f32[2304,512]{1,0:T(8,128)} %bitcast.32), slice={[128:2176], [0:512]} | slice | bytes 8388608
  69.4 5.4 %copy.10 = f32[2048,512]{0,1:T(8,128)} copy(f32[2048,512]{1,0:T(8,128)} %slice.25) | data formatting | bytes 8388608
  74.8 22.7 %all-gather.5.cloned.1.call-done = f32[2048,128]{1,0:T(8,128)} async-done(((f32[256,128]{1,0:T(8,128)}), f32[2048,128]{1,0:T(8,128)}) %all-gather.5.cloned.1.call-update) | async-done | bytes 1048592 | tf_op jit(solution)/shard_map/all_gather | solution.py:47
  97.6 270.4 %all-reduce.2.cloned.1.call-done = f32[128,512]{0,1:T(8,128)} async-done(((f32[128,512]{0,1:T(8,128)}), f32[128,512]{0,1:T(8,128)}) %all-reduce.2.cloned.1.call-update) | async-done | bytes 262160 | tf_op jit(solution)/shard_map/psum | solution.py:50
  368.0 8.0 %bitcast_subtract_fusion = f32[2048,512]{0,1:T(8,128)} fusion(f32[2048,512]{0,1:T(8,128)} %copy.10, f32[128,512]{0,1:T(8,128)} %all-reduce.2.cloned.1.call-done, f32[2048,128]{1,0:T(8,128)} %all-gather.5.cloned.1.call-done), kind=kOutput, calls=%fused_computation.1 | convolution fusion | flops 1611661312 | bytes 9699328 | tf_op jit(solution)/shard_map/dot_general | solution.py:51
  376.0 5.3 %copy.9 = f32[2048,512]{1,0:T(8,128)} copy(f32[2048,512]{0,1:T(8,128)} %bitcast_subtract_fusion) | data formatting | bytes 8388608 | tf_op jit(solution)/shard_map/sub | solution.py:51
Async XLA Ops:
  6.5 6.0 %copy-start = (f32[2048,128]{1,0:T(8,128)S(1)}, f32[2048,128]{1,0:T(8,128)}, u32[]{:S(2)}) copy-start(f32[2048,128]{1,0:T(8,128)} %param.9) | copy-start | bytes 3145732
  6.5 48.3 %all-gather.3.cloned.1.call-start = ((), (), s32[]{:S(2)}) async-start(), calls=%async_computation | async-start | bytes 1179648 | tf_op jit(solution)/shard_map/all_gather | solution.py:46
  7.3 90.3 %all-gather.5.cloned.1.call-start = ((), (), s32[]{:S(2)}) async-start(), calls=%async_computation.2 | async-start | bytes 1179648 | tf_op jit(solution)/shard_map/all_gather | solution.py:47
  7.3 5.3 %copy-start.3 = (f32[2048,512]{1,0:T(8,128)S(1)}, f32[2048,512]{1,0:T(8,128)}, u32[]{:S(2)}) copy-start(f32[2048,512]{1,0:T(8,128)} %param.7) | copy-start | bytes 12582916
  12.6 5.6 %copy-start.4 = (f32[2048,128]{1,0:T(8,128)S(1)}, f32[2048,128]{1,0:T(8,128)}, u32[]{:S(2)}) copy-start(f32[2048,128]{1,0:T(8,128)} %param.11) | copy-start | bytes 3145732
  12.6 5.6 %copy-start.5 = (f32[2048,128]{1,0:T(8,128)S(1)}, f32[2048,128]{1,0:T(8,128)}, u32[]{:S(2)}) copy-start(f32[2048,128]{1,0:T(8,128)} %param.10) | copy-start | bytes 3145732
  16.2 2.0 copy-start.1
  19.2 9.9 %collective-permute-start = (f32[128,768]{1,0:T(8,128)}, f32[128,768]{1,0:T(8,128)S(1)}, u32[]{:S(2)}, u32[]{:S(2)}) collective-permute-start(f32[128,768]{1,0:T(8,128)} %get-tuple-element.7), channel_id=1, source_target_pairs={{0,8},{8,16},{16,24},{24,32},{32,40},{40,48},{48,56},{56,64},{64,7... | collective-permute-start | bytes 1179656 | tf_op jit(solution)/shard_map/ppermute | solution.py:16
  24.1 9.7 %collective-permute-start.1 = (f32[128,768]{1,0:T(8,128)}, f32[128,768]{1,0:T(8,128)}, u32[]{:S(2)}, u32[]{:S(2)}) collective-permute-start(f32[128,768]{1,0:T(8,128)} %get-tuple-element.8), channel_id=1, source_target_pairs={{8,0},{16,8},{24,16},{32,24},{40,32},{48,40},{56,48},{64,56},{72,6... | collective-permute-start | bytes 1179656 | tf_op jit(solution)/shard_map/ppermute | solution.py:17
  26.0 342.0 %all-reduce.2.cloned.1.call-start = ((), (), s32[]{:S(2)}) async-start(), calls=%async_computation.1 | async-start | bytes 524288 | tf_op jit(solution)/shard_map/psum | solution.py:50
  37.4 2.2 copy-start.2
Sparse Core Ops, SparseCore 0:
  9.1 45.6 all-gather.2
  56.7 40.8 all-gather.4
  100.2 267.7 all-reduce.1
where the time goes:
time: 388 us
  waiting for transfers between devices  307 us (79%)
  matrix products  35.4 us (9%)
  local copies, waits for them, and re-layouts  19.6 us (5%)
  between operations  13.2 us (3%)
  starting transfers between devices  7.11 us (2%)
  other arithmetic  5.57 us (1%)
    psum x1, waiting for transfers between devices, local(): summed = lax.psum(partial_value, 'row')  270 us
    all_gather x1, waiting for transfers between devices, local(): lax.all_gather(panel_w, 'col', axis=0, tiled=True)  22.7 us
    unnamed x14, local copies, waits for them, and re-layouts  13.6 us
    dot_general x1, matrix products, local(): jnp.einsum('ik,ic->kc', rows_y, after_two, precision=highest)  9.86 us
    dot_general x2, matrix products, grouped(): update = jnp.einsum('gik,gkc->gic', wt_blocks, projected, precision=highest)  9.17 us
    dot_general x2, matrix products, grouped(): jnp.einsum('gik,gic->gkc', vec_blocks, blocks, precision=highest)  8.4 us
    dot_general x1, matrix products, local(): jnp.dot(rows_w, summed, precision=highest, preferred_element_type=jnp.flo...  7.99 us
  transfers between devices with their start and end apart: 5, of which 5 were waited for; matrix products, arithmetic and copies ran while one was open for 11% of the time, Pallas kernels for 0%

commit v1 on v0

v1 whole, which is shorter than its diff:
```python
import functools

import jax
import jax.numpy as jnp
from jax import lax
from jax.experimental import pallas as pl
from jax.experimental.pallas import tpu as pltpu
from jax.sharding import PartitionSpec as P

MESH = pl.DeviceIdType.MESH
f32, bf16 = jnp.float32, jnp.bfloat16
ROWS, COLS, B, G = 2048, 512, 128, 256
GROUPS = ROWS // G
SHARD = 256
Z, CHIPS, COL = 8, 16, 8

X, OWN_UP, OWN_DN, OTH_UP, OTH_DN, FWD_OWN_UP, FWD_OWN_DN, FWD_OTH_UP, FWD_OTH_DN = range(9)
KINDS = 9
FAR = [(1, 4), (1, 3), (1, 5), (1, 2), (1, 6), (0, 4), (1, 1), (1, 7), (0, 3), (0, 5), (1, 0), (0, 2), (0, 6), (0, 1), (0, 7)]


def split(x):
    high = x.astype(bf16)
    return high, (x - high.astype(f32)).astype(bf16)


def dot(a, b):
    return jnp.dot(a, b, preferred_element_type=f32)


def project(v, a):
    vh, vl = split(v.T)
    ah, al = split(a)
    return dot(vh, ah) + dot(vl, ah) + dot(vh, al)


def expand(w, p):
    wh, wl = split(w)
    ph, pll = split(p)
    return dot(jnp.concatenate([wh, wl], 1), jnp.concatenate([ph, ph], 0)) + dot(wh, pll)


def chain_kernel(
    e_ref, v0_ref, w0_ref, v1_ref, w1_ref, y_ref, w_ref,
    a_ref, wcat_ref, s_ref,
    v0, w0, v1, w1, ystage, yg, wg, halo_out, halo_in, total, half_out, half_in, mine, reduce_in, sums,
    in_sem, y_send, y_recv, w_send, w_recv, halo_send, halo_recv, core_send, core_recv, rs_send, rs_recv, ag_send, ag_recv,
    know_a, know_b, know_c,
):
    row, col = lax.axis_index("row"), lax.axis_index("col")
    x_hi, z, core = row // (2 * Z), (row // 2) % Z, row % 2
    chip = row // 2

    def row_of(xh, zz, cc):
        return xh * (2 * Z) + zz * 2 + cc

    def along(dx, dz):
        return ((x_hi + dx) % 2, (z + dz) % Z)

    other_col = col + 1 - 2 * (col % 2)
    up_col, down_col = (col + 2) % COL, (col + 6) % COL
    far_col = (col + 4) % COL
    to_x, to_up, to_down = (row, other_col), (row, up_col), (row, down_col)
    to_core = (row + 1 - 2 * core, col)
    next_row, prev_row = (row + 1) % (4 * Z), (row + 4 * Z - 1) % (4 * Z)
    to_next, to_prev = (next_row, col), (prev_row, col)
    to_side = (jnp.where(core == 0, prev_row, next_row), col)

    def chip_at(dx, dz):
        xh, zz = along(dx, dz)
        return (row_of(xh, zz, core), col)

    locals_ = []

    def fetch(src, dst):
        copy = pltpu.make_async_copy(src, dst, in_sem.at[len(locals_)])
        copy.start()
        locals_.append(copy)
        return copy

    get_y = fetch(y_ref, ystage)

    def part(src, dst, begin, size):
        return fetch(src.at[pl.ds(begin, size)], dst.at[pl.ds(begin, size)])

    get_e, get_edge = {}, {}
    for g in (0, GROUPS - 1):
        get_e[g] = part(e_ref, a_ref, G * g, G)
        get_edge[g] = [part(s, d, G * g, G) for s, d in ((v0_ref, v0), (w0_ref, w0), (v1_ref, v1))]

    barrier = pltpu.get_barrier_semaphore()
    near = [to_x, to_up, to_down, to_core, to_side, chip_at(0, 1), chip_at(0, Z - 1), chip_at(1, 0)]
    for device in near:
        pl.semaphore_signal(barrier, inc=1, device_id=device, device_id_type=MESH)

    inner = G * (GROUPS - 2)
    get_mid = [part(s, d, G, inner) for s, d in ((v0_ref, v0), (w0_ref, w0))]
    for g in range(1, 3):
        get_e[g] = part(e_ref, a_ref, G * g, G)
    get_mid1 = [part(s, d, G, inner) for s, d in ((v1_ref, v1), (w1_ref, w1))]
    for g in range(3, GROUPS - 1):
        get_e[g] = part(e_ref, a_ref, G * g, G)
    get_edge1 = [part(w1_ref, w1, G * g, G) for g in (0, GROUPS - 1)]
    get_w = fetch(w_ref, wg.at[pl.ds(pl.multiple_of(col * SHARD, SHARD), SHARD)])

    sent = []

    def send(src, dst, ssem, rsem, device):
        copy = pltpu.make_async_remote_copy(
            src_ref=src, dst_ref=dst, send_sem=ssem, recv_sem=rsem, device_id=device, device_id_type=MESH
        )
        copy.start()
        sent.append(copy)

    def arrived(dst, ssem, rsem):
        pltpu.make_async_remote_copy(
            src_ref=dst, dst_ref=dst, send_sem=ssem, recv_sem=rsem, device_id=to_x, device_id_type=MESH
        ).wait_recv()

    def gather(place, ssem, rsem):
        def out(kind, h, c, device):
            send(place(c, h), place(c, h), ssem.at[kind, h], rsem.at[kind, h], device)

        def wait(kind, h, c):
            arrived(place(c, h), ssem.at[kind, h], rsem.at[kind, h])

        def own():
            out(X, 0, col, to_x)
            out(OWN_UP, 0, col, to_up)
            out(OWN_DN, 1, col, to_down)
            out(X, 1, col, to_x)
            out(OWN_UP, 1, col, to_up)
            out(OWN_DN, 0, col, to_down)

        def relay(h):
            wait(X, h, other_col)
            out(OTH_UP, h, other_col, to_up)
            out(OTH_DN, h, other_col, to_down)

        def forward_own():
            wait(OWN_UP, 0, down_col)
            out(FWD_OWN_UP, 0, down_col, to_up)
            wait(OWN_DN, 1, up_col)
            out(FWD_OWN_DN, 1, up_col, to_down)

        def forward_other():
            wait(OTH_UP, 0, (other_col + 6) % COL)
            out(FWD_OTH_UP, 0, (other_col + 6) % COL, to_up)
            wait(OTH_DN, 1, (other_col + 2) % COL)
            out(FWD_OTH_DN, 1, (other_col + 2) % COL, to_down)

        def rest_own():
            wait(OWN_UP, 1, down_col)
            wait(OWN_DN, 0, up_col)

        def rest_other():
            wait(OTH_UP, 1, (other_col + 6) % COL)
            wait(OTH_DN, 0, (other_col + 2) % COL)

        def last_own():
            wait(FWD_OWN_UP, 0, far_col)
            wait(FWD_OWN_DN, 1, far_col)

        def last_other():
            wait(FWD_OTH_UP, 0, (other_col + 4) % COL)
            wait(FWD_OTH_DN, 1, (other_col + 4) % COL)

        return own, relay, forward_own, forward_other, rest_own, rest_other, last_own, last_other

    y_own, y_relay, y_fwd_own, y_fwd_oth, y_rest_own, y_rest_oth, y_last_own, y_last_oth = gather(
        lambda c, h: yg.at[c, pl.ds(64 * h, 64)], y_send, y_recv
    )
    w_own, w_relay, w_fwd_own, w_fwd_oth, w_rest_own, w_rest_oth, w_last_own, w_last_oth = gather(
        lambda c, h: wg.at[pl.ds(pl.multiple_of(c * SHARD + 128 * h, 128), 128)], w_send, w_recv
    )

    get_y.wait()
    yg[col] = ystage[...].T
    pl.semaphore_wait(barrier, len(near))
    y_own()
    for device in (chip_at(0, 1), chip_at(0, Z - 1), chip_at(1, 0)):
        pl.semaphore_signal(know_a, inc=1, device_id=device, device_id_type=MESH)

    def first(g):
        rows = pl.ds(g * G if isinstance(g, int) else pl.multiple_of(g * G, G), G)
        a = a_ref[rows, :]
        a_ref[rows, :] = a - expand(w0[rows, :], project(v0[rows, :], a))

    def second(g):
        begin = g * G + B
        rows = pl.ds(begin if isinstance(g, int) else pl.multiple_of(begin, B), G)
        a = a_ref[rows, :]
        a_ref[rows, :] = a - expand(w1[rows, :], project(v1[rows, :], a))

    top, bottom = pl.ds(0, B), pl.ds(ROWS - B, B)
    for g in (0, GROUPS - 1):
        get_e[g].wait()
        for copy in get_edge[g]:
            copy.wait()
        first(g)
        edge = top if g == 0 else bottom
        side = 0 if g == 0 else 1
        halo_out[side] = project(v1[edge, :], a_ref[edge, :])
        send(halo_out.at[side], halo_in.at[side], halo_send.at[side], halo_recv.at[side], to_prev if g == 0 else to_next)

    y_relay(0)
    for copy in get_mid:
        copy.wait()
    get_e[1].wait()
    first(1)
    y_relay(1)
    get_e[2].wait()
    first(2)
    for copy in get_mid1 + get_edge1:
        copy.wait()
    second(0)
    second(1)
    pl.semaphore_wait(know_a, 3)
    for device in (chip_at(0, 2), chip_at(0, Z - 2), chip_at(1, 0)):
        pl.semaphore_signal(know_b, inc=1, device_id=device, device_id_type=MESH)
    y_fwd_own()
    get_e[3].wait()
    get_e[4].wait()
    for g in (3, 4):
        first(g)
        second(g - 1)
    y_fwd_oth()
    get_w.wait()
    w_own()
    get_e[5].wait()
    get_e[6].wait()
    for g in (5, 6):
        first(g)
        second(g - 1)
    second(6)
    pl.semaphore_wait(know_b, 3)
    pl.semaphore_signal(know_c, inc=1, device_id=chip_at(1, 0), device_id_type=MESH)

    arrived(halo_in.at[1], halo_send.at[1], halo_recv.at[1])
    before = halo_out[0] + jnp.where(row == 0, 0.0, halo_in[1])
    a_ref[top, :] = a_ref[top, :] - expand(w1[top, :], before)
    arrived(halo_in.at[0], halo_send.at[0], halo_recv.at[0])
    after = halo_out[1] + jnp.where(row == 4 * Z - 1, 0.0, halo_in[0])
    a_ref[bottom, :] = a_ref[bottom, :] - expand(w1[bottom, :], after)

    def block(c):
        yh, yl = split(yg[c])
        ah, al = split(a_ref[pl.ds(pl.multiple_of(c * SHARD, SHARD), SHARD), :])
        return dot(yh, ah) + dot(yl, ah) + dot(yh, al)

    total[...] = block(col)
    total[...] += block(other_col)
    y_rest_own()
    total[...] += block(up_col)
    total[...] += block(down_col)
    w_relay(0)
    y_rest_oth()
    total[...] += block((other_col + 2) % COL)
    total[...] += block((other_col + 6) % COL)
    w_relay(1)
    y_last_own()
    total[...] += block(far_col)
    y_last_oth()
    total[...] += block((other_col + 4) % COL)

    half_out[...] = total[pl.ds(pl.multiple_of(64 * (1 - core), 64), 64), :]
    send(half_out, half_in, core_send.at[0], core_recv.at[0], to_core)
    pl.semaphore_wait(know_c, 1)
    arrived(half_in, core_send.at[0], core_recv.at[0])
    half = total[pl.ds(pl.multiple_of(64 * core, 64), 64), :] + half_in[...]
    for i in range(8):
        for j in range(2):
            mine[2 * i + j] = half[8 * i : 8 * i + 8, 256 * j : 256 * j + 256]
    for n, (dx, dz) in enumerate(FAR):
        xh, zz = along(dx, dz)
        send(mine.at[xh * Z + zz], reduce_in.at[n], rs_send.at[n], rs_recv.at[n], (row_of(xh, zz, core), col))
    w_fwd_own()
    for n in range(CHIPS - 1):
        arrived(reduce_in.at[n], rs_send.at[n], rs_recv.at[n])
    value = mine[chip]
    for n in range(CHIPS - 1):
        value += reduce_in[n]
    sums[core, chip] = value
    for n, (dx, dz) in enumerate(FAR):
        xh, zz = along(dx, dz)
        send(sums.at[core, chip], sums.at[core, chip], ag_send.at[n], ag_recv.at[n], (row_of(xh, zz, core), col))
    w_fwd_oth()
    w_rest_own()
    w_rest_oth()
    w_last_own()
    w_last_oth()
    for g in range(GROUPS):
        wh, wl = split(wg[pl.ds(g * G, G), :])
        wcat_ref[pl.ds(g * G, G), pl.ds(0, B)] = wh
        wcat_ref[pl.ds(g * G, G), pl.ds(B, B)] = wl
    for n, (dx, dz) in enumerate(FAR):
        xh, zz = along(dx, Z - dz)
        arrived(sums.at[core, xh * Z + zz], ag_send.at[n], ag_recv.at[n])
    send(sums.at[core], sums.at[core], core_send.at[1], core_recv.at[1], to_core)
    arrived(sums.at[1 - core], core_send.at[1], core_recv.at[1])
    for h in range(2):
        for i in range(8):
            for j in range(2):
                s_ref[pl.ds(64 * h + 8 * i, 8), pl.ds(256 * j, 256)] = sums[h, 2 * i + j]
    for copy in sent:
        copy.wait_send()


def chain(e, v0, w0, v1, w1, y, w):
    any_space = pl.BlockSpec(memory_space=pltpu.HBM)
    vmem = pl.BlockSpec(memory_space=pltpu.VMEM)
    dma = pltpu.SemaphoreType.DMA
    return pl.pallas_call(
        chain_kernel,
        out_shape=[
            pltpu.VMEM((ROWS, COLS), f32),
            pltpu.VMEM((ROWS, 2 * B), bf16),
            pltpu.VMEM((B, COLS), f32),
        ],
        in_specs=[any_space] * 7,
        out_specs=[vmem] * 3,
        scratch_shapes=[
            pltpu.VMEM((ROWS, B), f32),
            pltpu.VMEM((ROWS, B), f32),
            pltpu.VMEM((ROWS, B), f32),
            pltpu.VMEM((ROWS, B), f32),
            pltpu.VMEM((SHARD, B), f32),
            pltpu.VMEM((COL, B, SHARD), f32),
            pltpu.VMEM((ROWS, B), f32),
            pltpu.VMEM((2, B, COLS), f32),
            pltpu.VMEM((2, B, COLS), f32),
            pltpu.VMEM((B, COLS), f32),
            pltpu.VMEM((64, COLS), f32),
            pltpu.VMEM((64, COLS), f32),
            pltpu.VMEM((CHIPS, 8, 256), f32),
            pltpu.VMEM((CHIPS - 1, 8, 256), f32),
            pltpu.VMEM((2, CHIPS, 8, 256), f32),
            dma((32,)),
            dma((KINDS, 2)),
            dma((KINDS, 2)),
            dma((KINDS, 2)),
            dma((KINDS, 2)),
            dma((2,)),
            dma((2,)),
            dma((2,)),
            dma((2,)),
            dma((CHIPS - 1,)),
            dma((CHIPS - 1,)),
            dma((CHIPS - 1,)),
            dma((CHIPS - 1,)),
            pltpu.SemaphoreType.REGULAR,
            pltpu.SemaphoreType.REGULAR,
            pltpu.SemaphoreType.REGULAR,
        ],
        compiler_params=pltpu.CompilerParams(collective_id=0, has_side_effects=True, vmem_limit_bytes=40 << 20),
        name="chain",
    )(*(pltpu.with_memory_space_constraint(x, pltpu.HBM) for x in (e, v0, w0, v1, w1, y, w)))


def update_kernel(a_ref, wcat_ref, s_ref, o_ref, staged, sem):
    sh, sl = split(s_ref[...])
    twice = jnp.concatenate([sh, sh], 0)
    copies = []
    for g in range(GROUPS):
        rows = pl.ds(g * G, G)
        staged[rows, :] = a_ref[rows, :] - (dot(wcat_ref[rows, :], twice) + dot(wcat_ref[rows, :B], sl))
        copy = pltpu.make_async_copy(staged.at[rows], o_ref.at[rows], sem.at[g])
        copy.start()
        copies.append(copy)
    for copy in copies:
        copy.wait()


def update(a, wcat, s):
    a, wcat, s = (pltpu.with_memory_space_constraint(v, pltpu.VMEM) for v in (a, wcat, s))
    return pl.pallas_call(
        update_kernel,
        out_shape=jax.ShapeDtypeStruct((ROWS, COLS), f32),
        in_specs=[pl.BlockSpec(memory_space=pltpu.VMEM)] * 3,
        out_specs=pl.BlockSpec(memory_space=pl.ANY),
        scratch_shapes=[pltpu.VMEM((ROWS, COLS), f32), pltpu.SemaphoreType.DMA((GROUPS,))],
        compiler_params=pltpu.CompilerParams(vmem_limit_bytes=16 << 20),
        name="update",
    )(a, wcat, s)


def local(*operands):
    return update(*chain(*operands))


def solution(mesh):
    placed = (
        P("row", "col"),
        P("row", None),
        P("row", None),
        P("row", None),
        P("row", None),
        P(("row", "col"), None),
        P(("row", "col"), None),
    )
    return jax.shard_map(local, mesh=mesh, in_specs=placed, out_specs=P("row", "col"), check_vma=False)
```

time: 388 us -> 41.7 us (0.11)
  waiting for transfers between devices: 307 us -> 0 us
  Pallas kernels: 0 us -> 41.6 us
  matrix products: 35.4 us -> 0 us
  local copies, waits for them, and re-layouts: 19.6 us -> 0 us
  between operations: 13.2 us -> 0.01 us
  starting transfers between devices: 7.11 us -> 0 us
  other arithmetic: 5.57 us -> 0 us
    psum x1 -> x0, waiting for transfers between devices: 270 us -> none  [local(): summed = lax.psum(partial_value, 'row')]
    pallas_call x0 -> x2, Pallas kernels: none -> 41.6 us  [the longest x1 39.2 us: chain(): pl.pallas_call(chain_kernel, out_shape=[pltpu.VMEM((ROWS, COLS), f32), pl...]
    dot_general x6 -> x0, matrix products: 35.4 us -> none  [the longest x1 9.86 us: local(): jnp.einsum('ik,ic->kc', rows_y, after_two, precision=highest)]
    all_gather x2 -> x0, waiting for transfers between devices: 28.2 us -> none  [the longest x1 22.7 us: local(): lax.all_gather(panel_w, 'col', axis=0, tiled=True)]
    unnamed x14 -> x0, local copies, waits for them, and re-layouts: 13.6 us -> none
    ppermute x2 -> x0, waiting for transfers between devices: 7.52 us -> none  [the longest x1 4.69 us: with_halo(): after = lax.ppermute(first, axis, down)]
    ppermute x2 -> x0, starting transfers between devices: 6.84 us -> none  [the longest x1 4.92 us: with_halo(): before = lax.ppermute(last, axis, up)]
    sub x1 -> x0, local copies, waits for them, and re-layouts: 5.34 us -> none  [local(): after_two - jnp.dot(rows_w, summed, precision=highest, preferred_element_...]
  transfers between devices with their start and end apart: 5 -> 0, of which waited for: 5 -> 0; matrix products, arithmetic and copies ran while one was open for 11% -> 0% of each run, Pallas kernels for 0% -> 0%
where the time goes in v1:
time: 41.7 us; the launch traced here: 41.6 us
  Pallas kernels  41.6 us (100%)
    pallas_call x1, Pallas kernels, chain(): pl.pallas_call(chain_kernel, out_shape=[pltpu.VMEM((ROWS, COLS), f32), pl...  39.2 us
    pallas_call x1, Pallas kernels, update(): pl.pallas_call(update_kernel, out_shape=jax.ShapeDtypeStruct((ROWS, COLS)...  2.37 us

profile of v1, /device:TPU:1, one launch (start us, length us, event | category | flops | bytes accessed | tf_op | source)
XLA Modules:
  0.0 41.6 jit_solution(3048715612708501541)
XLA Ops:
  0.0 39.2 %chain.1 = (f32[2048,512]{1,0:T(8,128)S(1)}, bf16[2048,256]{1,0:T(8,128)(2,1)S(1)}, f32[128,512]{1,0:T(8,128)S(1)}) custom-call(f32[2048,512]{1,0:T(8,128)} %e_ref.1, f32[2048,128]{1,0:T(8,128)} %v0_ref.1, f32[2048,128]{1,0:T(8,128)} %w0_ref.1, f32[2048,128]{1,0:T(8,128)} %v1_ref.1, f32[2048,128]{1,0:T(8,128)} %w1_ref.1, f32[256,128]{1,0:T(8,128)} %y_ref.1, ...), custom_call_target="tpu_custom_call" | custom-call | tf_op jit(solution)/shard_map/chain/pallas_call | solution.py:313
  39.2 2.4 %update.1 = f32[2048,512]{1,0:T(8,128)} custom-call(f32[2048,512]{1,0:T(8,128)S(1)} %get-tuple-element.8.a_ref, bf16[2048,256]{1,0:T(8,128)(2,1)S(1)} %get-tuple-element.9.wcat_ref, f32[128,512]{1,0:T(8,128)S(1)} %get-tuple-element.10.s_ref), custom_call_target="tpu_custom_call" | custom-call | tf_op jit(solution)/shard_map/update/pallas_call | solution.py:376

commit v2 on v1

--- a/solution.py
+++ b/solution.py
@@ -14,8 +14,8 @@
 SHARD = 256
 Z, CHIPS, COL = 8, 16, 8
 
-X, OWN_UP, OWN_DN, OTH_UP, OTH_DN, FWD_OWN_UP, FWD_OWN_DN, FWD_OTH_UP, FWD_OTH_DN = range(9)
-KINDS = 9
+X, FAR_Y, UP, DOWN, X_UP, X_DOWN, FAR_X = range(7)
+KINDS = 7
 FAR = [(1, 4), (1, 3), (1, 5), (1, 2), (1, 6), (0, 4), (1, 1), (1, 7), (0, 3), (0, 5), (1, 0), (0, 2), (0, 6), (0, 1), (0, 7)]
 
 
@@ -60,15 +60,19 @@
     other_col = col + 1 - 2 * (col % 2)
     up_col, down_col = (col + 2) % COL, (col + 6) % COL
     far_col = (col + 4) % COL
-    to_x, to_up, to_down = (row, other_col), (row, up_col), (row, down_col)
+    to_x, to_up, to_down, to_far = (row, other_col), (row, up_col), (row, down_col), (row, far_col)
     to_core = (row + 1 - 2 * core, col)
     next_row, prev_row = (row + 1) % (4 * Z), (row + 4 * Z - 1) % (4 * Z)
     to_next, to_prev = (next_row, col), (prev_row, col)
-    to_side = (jnp.where(core == 0, prev_row, next_row), col)
 
     def chip_at(dx, dz):
         xh, zz = along(dx, dz)
         return (row_of(xh, zz, core), col)
+
+    barrier = pltpu.get_barrier_semaphore()
+    near = [to_x, to_up, to_down, to_far, to_core, chip_at(0, 1), chip_at(0, Z - 1), chip_at(1, 0)]
+    for device in near:
+        pl.semaphore_signal(barrier, inc=1, device_id=device, device_id_type=MESH)
 
     locals_ = []
 
@@ -87,11 +91,6 @@
     for g in (0, GROUPS - 1):
         get_e[g] = part(e_ref, a_ref, G * g, G)
         get_edge[g] = [part(s, d, G * g, G) for s, d in ((v0_ref, v0), (w0_ref, w0), (v1_ref, v1))]
-
-    barrier = pltpu.get_barrier_semaphore()
-    near = [to_x, to_up, to_down, to_core, to_side, chip_at(0, 1), chip_at(0, Z - 1), chip_at(1, 0)]
-    for device in near:
-        pl.semaphore_signal(barrier, inc=1, device_id=device, device_id_type=MESH)
 
     inner = G * (GROUPS - 2)
     get_mid = [part(s, d, G, inner) for s, d in ((v0_ref, v0), (w0_ref, w0))]
@@ -117,7 +116,7 @@
             src_ref=dst, dst_ref=dst, send_sem=ssem, recv_sem=rsem, device_id=to_x, device_id_type=MESH
         ).wait_recv()
 
-    def gather(place, ssem, rsem):
+    def gather(pieces, place, ssem, rsem):
         def out(kind, h, c, device):
             send(place(c, h), place(c, h), ssem.at[kind, h], rsem.at[kind, h], device)
 
@@ -125,60 +124,50 @@
             arrived(place(c, h), ssem.at[kind, h], rsem.at[kind, h])
 
         def own():
-            out(X, 0, col, to_x)
-            out(OWN_UP, 0, col, to_up)
-            out(OWN_DN, 1, col, to_down)
-            out(X, 1, col, to_x)
-            out(OWN_UP, 1, col, to_up)
-            out(OWN_DN, 0, col, to_down)
+            for h in range(pieces):
+                out(FAR_Y, h, col, to_far)
+                out(X, h, col, to_x)
+            for h in range(pieces):
+                out(UP, h, col, to_up)
+                out(DOWN, h, col, to_down)
 
         def relay(h):
             wait(X, h, other_col)
-            out(OTH_UP, h, other_col, to_up)
-            out(OTH_DN, h, other_col, to_down)
-
-        def forward_own():
-            wait(OWN_UP, 0, down_col)
-            out(FWD_OWN_UP, 0, down_col, to_up)
-            wait(OWN_DN, 1, up_col)
-            out(FWD_OWN_DN, 1, up_col, to_down)
-
-        def forward_other():
-            wait(OTH_UP, 0, (other_col + 6) % COL)
-            out(FWD_OTH_UP, 0, (other_col + 6) % COL, to_up)
-            wait(OTH_DN, 1, (other_col + 2) % COL)
-            out(FWD_OTH_DN, 1, (other_col + 2) % COL, to_down)
+            out(X_UP, h, other_col, to_up)
+            out(X_DOWN, h, other_col, to_down)
+
+        def relay_far(h):
+            wait(FAR_Y, h, far_col)
+            out(FAR_X, h, far_col, to_x)
 
         def rest_own():
-            wait(OWN_UP, 1, down_col)
-            wait(OWN_DN, 0, up_col)
+            for h in range(pieces):
+                wait(UP, h, down_col)
+                wait(DOWN, h, up_col)
 
         def rest_other():
-            wait(OTH_UP, 1, (other_col + 6) % COL)
-            wait(OTH_DN, 0, (other_col + 2) % COL)
-
-        def last_own():
-            wait(FWD_OWN_UP, 0, far_col)
-            wait(FWD_OWN_DN, 1, far_col)
-
-        def last_other():
-            wait(FWD_OTH_UP, 0, (other_col + 4) % COL)
-            wait(FWD_OTH_DN, 1, (other_col + 4) % COL)
-
-        return own, relay, forward_own, forward_other, rest_own, rest_other, last_own, last_other
-
-    y_own, y_relay, y_fwd_own, y_fwd_oth, y_rest_own, y_rest_oth, y_last_own, y_last_oth = gather(
-        lambda c, h: yg.at[c, pl.ds(64 * h, 64)], y_send, y_recv
+            for h in range(pieces):
+                wait(X_UP, h, (other_col + 6) % COL)
+                wait(X_DOWN, h, (other_col + 2) % COL)
+
+        def rest_far():
+            for h in range(pieces):
+                wait(FAR_X, h, (other_col + 4) % COL)
+
+        return own, relay, relay_far, rest_own, rest_other, rest_far
+
+    y_own, y_relay, y_relay_far, y_rest_own, y_rest_other, y_rest_far = gather(
+        2, lambda c, h: yg.at[c, pl.ds(64 * h, 64)], y_send, y_recv
     )
-    w_own, w_relay, w_fwd_own, w_fwd_oth, w_rest_own, w_rest_oth, w_last_own, w_last_oth = gather(
-        lambda c, h: wg.at[pl.ds(pl.multiple_of(c * SHARD + 128 * h, 128), 128)], w_send, w_recv
+    w_own, w_relay, w_relay_far, w_rest_own, w_rest_other, w_rest_far = gather(
+        1, lambda c, h: wg.at[pl.ds(pl.multiple_of(c * SHARD, SHARD), SHARD)], w_send, w_recv
     )
 
     get_y.wait()
     yg[col] = ystage[...].T
     pl.semaphore_wait(barrier, len(near))
     y_own()
-    for device in (chip_at(0, 1), chip_at(0, Z - 1), chip_at(1, 0)):
+    for device in (chip_at(0, 1), chip_at(0, Z - 1), chip_at(1, 0), to_core):
         pl.semaphore_signal(know_a, inc=1, device_id=device, device_id_type=MESH)
 
     def first(g):
@@ -201,7 +190,10 @@
         edge = top if g == 0 else bottom
         side = 0 if g == 0 else 1
         halo_out[side] = project(v1[edge, :], a_ref[edge, :])
-        send(halo_out.at[side], halo_in.at[side], halo_send.at[side], halo_recv.at[side], to_prev if g == 0 else to_next)
+
+    pl.semaphore_wait(know_a, 4)
+    for device in (chip_at(0, 2), chip_at(0, Z - 2), chip_at(1, 0)):
+        pl.semaphore_signal(know_b, inc=1, device_id=device, device_id_type=MESH)
 
     y_relay(0)
     for copy in get_mid:
@@ -215,16 +207,17 @@
         copy.wait()
     second(0)
     second(1)
-    pl.semaphore_wait(know_a, 3)
-    for device in (chip_at(0, 2), chip_at(0, Z - 2), chip_at(1, 0)):
-        pl.semaphore_signal(know_b, inc=1, device_id=device, device_id_type=MESH)
-    y_fwd_own()
+    pl.semaphore_wait(know_b, 3)
+    pl.semaphore_signal(know_c, inc=1, device_id=chip_at(1, 0), device_id_type=MESH)
+    for side, device in ((0, to_prev), (1, to_next)):
+        send(halo_out.at[side], halo_in.at[side], halo_send.at[side], halo_recv.at[side], device)
+    y_relay_far(0)
     get_e[3].wait()
     get_e[4].wait()
     for g in (3, 4):
         first(g)
         second(g - 1)
-    y_fwd_oth()
+    y_relay_far(1)
     get_w.wait()
     w_own()
     get_e[5].wait()
@@ -233,8 +226,6 @@
         first(g)
         second(g - 1)
     second(6)
-    pl.semaphore_wait(know_b, 3)
-    pl.semaphore_signal(know_c, inc=1, device_id=chip_at(1, 0), device_id_type=MESH)
 
     arrived(halo_in.at[1], halo_send.at[1], halo_recv.at[1])
     before = halo_out[0] + jnp.where(row == 0, 0.0, halo_in[1])
@@ -250,17 +241,15 @@
 
     total[...] = block(col)
     total[...] += block(other_col)
+    total[...] += block(far_col)
     y_rest_own()
     total[...] += block(up_col)
     total[...] += block(down_col)
     w_relay(0)
-    y_rest_oth()
+    y_rest_other()
     total[...] += block((other_col + 2) % COL)
     total[...] += block((other_col + 6) % COL)
-    w_relay(1)
-    y_last_own()
-    total[...] += block(far_col)
-    y_last_oth()
+    y_rest_far()
     total[...] += block((other_col + 4) % COL)
 
     half_out[...] = total[pl.ds(pl.multiple_of(64 * (1 - core), 64), 64), :]
@@ -274,7 +263,7 @@
     for n, (dx, dz) in enumerate(FAR):
         xh, zz = along(dx, dz)
         send(mine.at[xh * Z + zz], reduce_in.at[n], rs_send.at[n], rs_recv.at[n], (row_of(xh, zz, core), col))
-    w_fwd_own()
+    w_relay_far(0)
     for n in range(CHIPS - 1):
         arrived(reduce_in.at[n], rs_send.at[n], rs_recv.at[n])
     value = mine[chip]
@@ -284,11 +273,9 @@
     for n, (dx, dz) in enumerate(FAR):
         xh, zz = along(dx, dz)
         send(sums.at[core, chip], sums.at[core, chip], ag_send.at[n], ag_recv.at[n], (row_of(xh, zz, core), col))
-    w_fwd_oth()
     w_rest_own()
-    w_rest_oth()
-    w_last_own()
-    w_last_oth()
+    w_rest_other()
+    w_rest_far()
     for g in range(GROUPS):
         wh, wl = split(wg[pl.ds(g * G, G), :])
         wcat_ref[pl.ds(g * G, G), pl.ds(0, B)] = wh

time: 41.7 us -> 42.6 us (1.022)
  Pallas kernels: 41.6 us -> 42.5 us
    pallas_call x1, Pallas kernels: 39.2 us -> 40.1 us  [chain(): pl.pallas_call(chain_kernel, out_shape=[pltpu.VMEM((ROWS, COLS), f32), pl...]
where the time goes in v2:
time: 42.6 us; the launch traced here: 42.5 us
  Pallas kernels  42.5 us (100%)
    pallas_call x1, Pallas kernels, chain(): pl.pallas_call(chain_kernel, out_shape=[pltpu.VMEM((ROWS, COLS), f32), pl...  40.1 us
    pallas_call x1, Pallas kernels, update(): pl.pallas_call(update_kernel, out_shape=jax.ShapeDtypeStruct((ROWS, COLS)...  2.37 us

profile of v2, /device:TPU:1, one launch (start us, length us, event | category | flops | bytes accessed | tf_op | source)
XLA Modules:
  0.0 42.5 jit_solution(4978701024475033)
XLA Ops:
  0.0 40.1 %chain.1 = (f32[2048,512]{1,0:T(8,128)S(1)}, bf16[2048,256]{1,0:T(8,128)(2,1)S(1)}, f32[128,512]{1,0:T(8,128)S(1)}) custom-call(f32[2048,512]{1,0:T(8,128)} %e_ref.1, f32[2048,128]{1,0:T(8,128)} %v0_ref.1, f32[2048,128]{1,0:T(8,128)} %w0_ref.1, f32[2048,128]{1,0:T(8,128)} %v1_ref.1, f32[2048,128]{1,0:T(8,128)} %w1_ref.1, f32[256,128]{1,0:T(8,128)} %y_ref.1, ...), custom_call_target="tpu_custom_call" | custom-call | tf_op jit(solution)/shard_map/chain/pallas_call | solution.py:300
  40.1 2.4 %update.1 = f32[2048,512]{1,0:T(8,128)} custom-call(f32[2048,512]{1,0:T(8,128)S(1)} %get-tuple-element.8.a_ref, bf16[2048,256]{1,0:T(8,128)(2,1)S(1)} %get-tuple-element.9.wcat_ref, f32[128,512]{1,0:T(8,128)S(1)} %get-tuple-element.10.s_ref), custom_call_target="tpu_custom_call" | custom-call | tf_op jit(solution)/shard_map/update/pallas_call | solution.py:363

commit v3 on v2

--- a/solution.py
+++ b/solution.py
@@ -28,24 +28,30 @@
     return jnp.dot(a, b, preferred_element_type=f32)
 
 
+def thrice(x, a):
+    m = x.shape[0]
+    xh, xl = split(x)
+    ah, al = split(a)
+    both = dot(jnp.concatenate([xh, xl], 0), ah)
+    return both[:m] + both[m:] + dot(xh, al)
+
+
 def project(v, a):
-    vh, vl = split(v.T)
-    ah, al = split(a)
-    return dot(vh, ah) + dot(vl, ah) + dot(vh, al)
+    return thrice(v.T, a)
 
 
 def expand(w, p):
     wh, wl = split(w)
-    ph, pll = split(p)
-    return dot(jnp.concatenate([wh, wl], 1), jnp.concatenate([ph, ph], 0)) + dot(wh, pll)
+    ph, pl_ = split(p)
+    return dot(jnp.concatenate([wh, wl, wh], 1), jnp.concatenate([ph, ph, pl_], 0))
 
 
 def chain_kernel(
     e_ref, v0_ref, w0_ref, v1_ref, w1_ref, y_ref, w_ref,
     a_ref, wcat_ref, s_ref,
-    v0, w0, v1, w1, ystage, yg, wg, halo_out, halo_in, total, half_out, half_in, mine, reduce_in, sums,
+    v0, w0, v1, w1, ystage, yg, wg, halo_out, halo_in, total, half_out, half_in, mine, reduce_in, sums, late_high, late_low,
     in_sem, y_send, y_recv, w_send, w_recv, halo_send, halo_recv, core_send, core_recv, rs_send, rs_recv, ag_send, ag_recv,
-    know_a, know_b, know_c,
+    know_a, know_b, know_c, know_d,
 ):
     row, col = lax.axis_index("row"), lax.axis_index("col")
     x_hi, z, core = row // (2 * Z), (row // 2) % Z, row % 2
@@ -63,7 +69,7 @@
     to_x, to_up, to_down, to_far = (row, other_col), (row, up_col), (row, down_col), (row, far_col)
     to_core = (row + 1 - 2 * core, col)
     next_row, prev_row = (row + 1) % (4 * Z), (row + 4 * Z - 1) % (4 * Z)
-    to_next, to_prev = (next_row, col), (prev_row, col)
+    to_side = (jnp.where(core == 0, prev_row, next_row), col)
 
     def chip_at(dx, dz):
         xh, zz = along(dx, dz)
@@ -163,106 +169,120 @@
         1, lambda c, h: wg.at[pl.ds(pl.multiple_of(c * SHARD, SHARD), SHARD)], w_send, w_recv
     )
 
+    def apply(v, w, begins):
+        old = [a_ref[pl.ds(i, G), :] for i in begins]
+        inner_ = [project(v[pl.ds(i, G), :], a) for i, a in zip(begins, old)]
+        new = [a - expand(w[pl.ds(i, G), :], p) for i, a, p in zip(begins, old, inner_)]
+        for i, a in zip(begins, new):
+            a_ref[pl.ds(i, G), :] = a
+
+    def first(*groups):
+        apply(v0, w0, [g * G for g in groups])
+
+    def second(*groups):
+        apply(v1, w1, [g * G + B for g in groups])
+
+    def send_halo(side, device):
+        send(halo_out.at[side], halo_in.at[side], halo_send.at[side], halo_recv.at[side], device)
+
+    edges = (pl.ds(0, B), pl.ds(ROWS - B, B))
     get_y.wait()
     yg[col] = ystage[...].T
-    pl.semaphore_wait(barrier, len(near))
-    y_own()
-    for device in (chip_at(0, 1), chip_at(0, Z - 1), chip_at(1, 0), to_core):
-        pl.semaphore_signal(know_a, inc=1, device_id=device, device_id_type=MESH)
-
-    def first(g):
-        rows = pl.ds(g * G if isinstance(g, int) else pl.multiple_of(g * G, G), G)
-        a = a_ref[rows, :]
-        a_ref[rows, :] = a - expand(w0[rows, :], project(v0[rows, :], a))
-
-    def second(g):
-        begin = g * G + B
-        rows = pl.ds(begin if isinstance(g, int) else pl.multiple_of(begin, B), G)
-        a = a_ref[rows, :]
-        a_ref[rows, :] = a - expand(w1[rows, :], project(v1[rows, :], a))
-
-    top, bottom = pl.ds(0, B), pl.ds(ROWS - B, B)
     for g in (0, GROUPS - 1):
         get_e[g].wait()
         for copy in get_edge[g]:
             copy.wait()
-        first(g)
-        edge = top if g == 0 else bottom
-        side = 0 if g == 0 else 1
-        halo_out[side] = project(v1[edge, :], a_ref[edge, :])
-
-    pl.semaphore_wait(know_a, 4)
+    first(0, GROUPS - 1)
+    for side in range(2):
+        halo_out[side] = project(v1[edges[side], :], a_ref[edges[side], :])
+    pl.semaphore_wait(barrier, len(near))
+    y_own()
+    for device in (chip_at(0, 1), chip_at(0, Z - 1), chip_at(1, 0)):
+        pl.semaphore_signal(know_a, inc=1, device_id=device, device_id_type=MESH)
+    send_halo(1 - core, to_core)
+    for copy in get_mid + [get_e[1], get_e[2]]:
+        copy.wait()
+    first(1, 2)
+    for copy in get_mid1 + get_edge1:
+        copy.wait()
+    second(0, 1)
+    pl.semaphore_wait(know_a, 3)
     for device in (chip_at(0, 2), chip_at(0, Z - 2), chip_at(1, 0)):
         pl.semaphore_signal(know_b, inc=1, device_id=device, device_id_type=MESH)
-
+    pl.semaphore_signal(know_d, inc=1, device_id=to_core, device_id_type=MESH)
     y_relay(0)
-    for copy in get_mid:
-        copy.wait()
-    get_e[1].wait()
-    first(1)
-    y_relay(1)
-    get_e[2].wait()
-    first(2)
-    for copy in get_mid1 + get_edge1:
-        copy.wait()
-    second(0)
-    second(1)
-    pl.semaphore_wait(know_b, 3)
-    pl.semaphore_signal(know_c, inc=1, device_id=chip_at(1, 0), device_id_type=MESH)
-    for side, device in ((0, to_prev), (1, to_next)):
-        send(halo_out.at[side], halo_in.at[side], halo_send.at[side], halo_recv.at[side], device)
-    y_relay_far(0)
+    pl.semaphore_wait(know_d, 1)
+    send_halo(core, to_side)
     get_e[3].wait()
     get_e[4].wait()
-    for g in (3, 4):
-        first(g)
-        second(g - 1)
+    first(3, 4)
+    y_relay(1)
+    second(2, 3)
+    y_relay_far(0)
+    get_e[5].wait()
+    get_e[6].wait()
+    first(5, 6)
     y_relay_far(1)
     get_w.wait()
     w_own()
-    get_e[5].wait()
-    get_e[6].wait()
-    for g in (5, 6):
-        first(g)
-        second(g - 1)
+    pl.semaphore_wait(know_b, 3)
+    pl.semaphore_signal(know_c, inc=1, device_id=chip_at(1, 0), device_id_type=MESH)
+    second(4, 5)
     second(6)
-
-    arrived(halo_in.at[1], halo_send.at[1], halo_recv.at[1])
-    before = halo_out[0] + jnp.where(row == 0, 0.0, halo_in[1])
-    a_ref[top, :] = a_ref[top, :] - expand(w1[top, :], before)
-    arrived(halo_in.at[0], halo_send.at[0], halo_recv.at[0])
-    after = halo_out[1] + jnp.where(row == 4 * Z - 1, 0.0, halo_in[0])
-    a_ref[bottom, :] = a_ref[bottom, :] - expand(w1[bottom, :], after)
+    for side in range(2):
+        a_ref[edges[side], :] -= expand(w1[edges[side], :], halo_out[side])
+
+    def rows_of(c):
+        return pl.ds(pl.multiple_of(c * SHARD, SHARD), SHARD)
 
     def block(c):
-        yh, yl = split(yg[c])
-        ah, al = split(a_ref[pl.ds(pl.multiple_of(c * SHARD, SHARD), SHARD), :])
-        return dot(yh, ah) + dot(yl, ah) + dot(yh, al)
-
-    total[...] = block(col)
-    total[...] += block(other_col)
-    total[...] += block(far_col)
+        return thrice(yg[c], a_ref[rows_of(c), :])
+
+    total[...] = block(col) + block(other_col) + block(far_col)
     y_rest_own()
-    total[...] += block(up_col)
-    total[...] += block(down_col)
+    total[...] += block(up_col) + block(down_col)
+
+    for side in (1, 0):
+        edge, c, offset = edges[1 - side], (COL - 1) * (1 - side), (SHARD - B) * (1 - side)
+        arrived(halo_in.at[side], halo_send.at[side], halo_recv.at[side])
+        other = jnp.where(row == (4 * Z - 1, 0)[side], 0.0, halo_in[side])
+        a_ref[edge, :] -= expand(w1[edge, :], other)
+
+        @pl.when((col % 2 == c % 2) | (other_col == c))
+        def _():
+            total[...] -= expand(thrice(yg[c, :, pl.ds(offset, B)], w1[edge, :]), other)
+
+    late = (other_col + 4) % COL, (other_col + 2) % COL, (other_col + 6) % COL
+    for i, c in enumerate(late):
+        late_high[i], late_low[i] = split(a_ref[rows_of(c), :])
+
+    halves = [pl.ds(pl.multiple_of(256 * ((z + n) % 2), 256), 256) for n in range(2)]
+
+    def late_block(i, y, columns):
+        both = dot(jnp.concatenate(y, 0), late_high[i, :, columns])
+        return both[:B] + both[B:] + dot(y[0], late_low[i, :, columns])
+
+    y_rest_far()
+    y = split(yg[late[0]])
+    for columns in halves:
+        total[:, columns] += late_block(0, y, columns)
+    y_rest_other()
+    y1, y2 = split(yg[late[1]]), split(yg[late[2]])
+    for n, columns in enumerate(halves):
+        total[:, columns] += late_block(1, y1, columns) + late_block(2, y2, columns)
+        half_out[n] = total[pl.ds(pl.multiple_of(64 * (1 - core), 64), 64), columns]
+        send(half_out.at[n], half_in.at[n], core_send.at[n], core_recv.at[n], to_core)
+    pl.semaphore_wait(know_c, 1)
+    for n, columns in enumerate(halves):
+        arrived(half_in.at[n], core_send.at[n], core_recv.at[n])
+        half = total[pl.ds(pl.multiple_of(64 * core, 64), 64), columns] + half_in[n]
+        for i in range(8):
+            mine[2 * i + (z + n) % 2] = half[8 * i : 8 * i + 8]
+        for m, (dx, dz) in enumerate(FAR):
+            if dz % 2 == n:
+                xh, zz = along(dx, dz)
+                send(mine.at[xh * Z + zz], reduce_in.at[m], rs_send.at[m], rs_recv.at[m], chip_at(dx, dz))
     w_relay(0)
-    y_rest_other()
-    total[...] += block((other_col + 2) % COL)
-    total[...] += block((other_col + 6) % COL)
-    y_rest_far()
-    total[...] += block((other_col + 4) % COL)
-
-    half_out[...] = total[pl.ds(pl.multiple_of(64 * (1 - core), 64), 64), :]
-    send(half_out, half_in, core_send.at[0], core_recv.at[0], to_core)
-    pl.semaphore_wait(know_c, 1)
-    arrived(half_in, core_send.at[0], core_recv.at[0])
-    half = total[pl.ds(pl.multiple_of(64 * core, 64), 64), :] + half_in[...]
-    for i in range(8):
-        for j in range(2):
-            mine[2 * i + j] = half[8 * i : 8 * i + 8, 256 * j : 256 * j + 256]
-    for n, (dx, dz) in enumerate(FAR):
-        xh, zz = along(dx, dz)
-        send(mine.at[xh * Z + zz], reduce_in.at[n], rs_send.at[n], rs_recv.at[n], (row_of(xh, zz, core), col))
     w_relay_far(0)
     for n in range(CHIPS - 1):
         arrived(reduce_in.at[n], rs_send.at[n], rs_recv.at[n])
@@ -271,20 +291,25 @@
         value += reduce_in[n]
     sums[core, chip] = value
     for n, (dx, dz) in enumerate(FAR):
-        xh, zz = along(dx, dz)
-        send(sums.at[core, chip], sums.at[core, chip], ag_send.at[n], ag_recv.at[n], (row_of(xh, zz, core), col))
+        send(sums.at[core, chip], sums.at[core, chip], ag_send.at[n], ag_recv.at[n], chip_at(dx, dz))
     w_rest_own()
+    w_rest_far()
     w_rest_other()
-    w_rest_far()
     for g in range(GROUPS):
         wh, wl = split(wg[pl.ds(g * G, G), :])
         wcat_ref[pl.ds(g * G, G), pl.ds(0, B)] = wh
         wcat_ref[pl.ds(g * G, G), pl.ds(B, B)] = wl
-    for n, (dx, dz) in enumerate(FAR):
-        xh, zz = along(dx, Z - dz)
-        arrived(sums.at[core, xh * Z + zz], ag_send.at[n], ag_recv.at[n])
-    send(sums.at[core], sums.at[core], core_send.at[1], core_recv.at[1], to_core)
-    arrived(sums.at[1 - core], core_send.at[1], core_recv.at[1])
+        wcat_ref[pl.ds(g * G, G), pl.ds(2 * B, B)] = wh
+    planes = [pl.ds(pl.multiple_of(Z * ((x_hi + dx) % 2), Z), Z) for dx in range(2)]
+    for side in range(2):
+        for n, (dx, dz) in enumerate(FAR):
+            if dx == side:
+                xh, zz = along(dx, Z - dz)
+                arrived(sums.at[core, xh * Z + zz], ag_send.at[n], ag_recv.at[n])
+        whole = sums.at[core, planes[side]]
+        send(whole, whole, core_send.at[2 + side], core_recv.at[2 + side], to_core)
+    for side in range(2):
+        arrived(sums.at[1 - core, planes[side]], core_send.at[2 + side], core_recv.at[2 + side])
     for h in range(2):
         for i in range(8):
             for j in range(2):
@@ -301,7 +326,7 @@
         chain_kernel,
         out_shape=[
             pltpu.VMEM((ROWS, COLS), f32),
-            pltpu.VMEM((ROWS, 2 * B), bf16),
+            pltpu.VMEM((ROWS, 3 * B), bf16),
             pltpu.VMEM((B, COLS), f32),
         ],
         in_specs=[any_space] * 7,
@@ -317,11 +342,13 @@
             pltpu.VMEM((2, B, COLS), f32),
             pltpu.VMEM((2, B, COLS), f32),
             pltpu.VMEM((B, COLS), f32),
-            pltpu.VMEM((64, COLS), f32),
-            pltpu.VMEM((64, COLS), f32),
+            pltpu.VMEM((2, 64, 256), f32),
+            pltpu.VMEM((2, 64, 256), f32),
             pltpu.VMEM((CHIPS, 8, 256), f32),
             pltpu.VMEM((CHIPS - 1, 8, 256), f32),
             pltpu.VMEM((2, CHIPS, 8, 256), f32),
+            pltpu.VMEM((3, SHARD, COLS), bf16),
+            pltpu.VMEM((3, SHARD, COLS), bf16),
             dma((32,)),
             dma((KINDS, 2)),
             dma((KINDS, 2)),
@@ -329,8 +356,8 @@
             dma((KINDS, 2)),
             dma((2,)),
             dma((2,)),
-            dma((2,)),
-            dma((2,)),
+            dma((4,)),
+            dma((4,)),
             dma((CHIPS - 1,)),
             dma((CHIPS - 1,)),
             dma((CHIPS - 1,)),
@@ -338,6 +365,7 @@
             pltpu.SemaphoreType.REGULAR,
             pltpu.SemaphoreType.REGULAR,
             pltpu.SemaphoreType.REGULAR,
+            pltpu.SemaphoreType.REGULAR,
         ],
         compiler_params=pltpu.CompilerParams(collective_id=0, has_side_effects=True, vmem_limit_bytes=40 << 20),
         name="chain",
@@ -346,11 +374,11 @@
 
 def update_kernel(a_ref, wcat_ref, s_ref, o_ref, staged, sem):
     sh, sl = split(s_ref[...])
-    twice = jnp.concatenate([sh, sh], 0)
+    s = jnp.concatenate([sh, sh, sl], 0)
     copies = []
     for g in range(GROUPS):
         rows = pl.ds(g * G, G)
-        staged[rows, :] = a_ref[rows, :] - (dot(wcat_ref[rows, :], twice) + dot(wcat_ref[rows, :B], sl))
+        staged[rows, :] = a_ref[rows, :] - dot(wcat_ref[rows, :], s)
         copy = pltpu.make_async_copy(staged.at[rows], o_ref.at[rows], sem.at[g])
         copy.start()
         copies.append(copy)

time: 42.6 us -> 40.1 us (0.941)
  Pallas kernels: 42.5 us -> 40 us
    pallas_call x1, Pallas kernels: 40.1 us -> 37.6 us  [chain(): pl.pallas_call(chain_kernel, out_shape=[pltpu.VMEM((ROWS, COLS), f32), pl...]
where the time goes in v3:
time: 40.1 us; the launch traced here: 40 us
  Pallas kernels  40 us (100%)
    pallas_call x1, Pallas kernels, chain(): pl.pallas_call(chain_kernel, out_shape=[pltpu.VMEM((ROWS, COLS), f32), pl...  37.6 us
    pallas_call x1, Pallas kernels, update(): pl.pallas_call(update_kernel, out_shape=jax.ShapeDtypeStruct((ROWS, COLS)...  2.37 us

profile of v3, /device:TPU:1, one launch (start us, length us, event | category | flops | bytes accessed | tf_op | source)
XLA Modules:
  0.0 40.0 jit_solution(3984093669238946856)
XLA Ops:
  0.0 37.6 %chain.1 = (f32[2048,512]{1,0:T(8,128)S(1)}, bf16[2048,384]{1,0:T(8,128)(2,1)S(1)}, f32[128,512]{1,0:T(8,128)S(1)}) custom-call(f32[2048,512]{1,0:T(8,128)} %e_ref.1, f32[2048,128]{1,0:T(8,128)} %v0_ref.1, f32[2048,128]{1,0:T(8,128)} %w0_ref.1, f32[2048,128]{1,0:T(8,128)} %v1_ref.1, f32[2048,128]{1,0:T(8,128)} %w1_ref.1, f32[256,128]{1,0:T(8,128)} %y_ref.1, ...), custom_call_target="tpu_custom_call" | custom-call | tf_op jit(solution)/shard_map/chain/pallas_call | solution.py:325
  37.6 2.4 %update.1 = f32[2048,512]{1,0:T(8,128)} custom-call(f32[2048,512]{1,0:T(8,128)S(1)} %get-tuple-element.8.a_ref, bf16[2048,384]{1,0:T(8,128)(2,1)S(1)} %get-tuple-element.9.wcat_ref, f32[128,512]{1,0:T(8,128)S(1)} %get-tuple-element.10.s_ref), custom_call_target="tpu_custom_call" | custom-call | tf_op jit(solution)/shard_map/update/pallas_call | solution.py:391

commit v4 on v3

--- a/solution.py
+++ b/solution.py
@@ -13,6 +13,7 @@
 GROUPS = ROWS // G
 SHARD = 256
 Z, CHIPS, COL = 8, 16, 8
+PARTS = 16
 
 X, FAR_Y, UP, DOWN, X_UP, X_DOWN, FAR_X = range(7)
 KINDS = 7
@@ -300,6 +301,9 @@
         wcat_ref[pl.ds(g * G, G), pl.ds(0, B)] = wh
         wcat_ref[pl.ds(g * G, G), pl.ds(B, B)] = wl
         wcat_ref[pl.ds(g * G, G), pl.ds(2 * B, B)] = wh
+    for copy in sent:
+        copy.wait_send()
+    done = len(sent)
     planes = [pl.ds(pl.multiple_of(Z * ((x_hi + dx) % 2), Z), Z) for dx in range(2)]
     for side in range(2):
         for n, (dx, dz) in enumerate(FAR):
@@ -314,7 +318,7 @@
         for i in range(8):
             for j in range(2):
                 s_ref[pl.ds(64 * h + 8 * i, 8), pl.ds(256 * j, 256)] = sums[h, 2 * i + j]
-    for copy in sent:
+    for copy in sent[done:]:
         copy.wait_send()
 
 
@@ -376,8 +380,8 @@
     sh, sl = split(s_ref[...])
     s = jnp.concatenate([sh, sh, sl], 0)
     copies = []
-    for g in range(GROUPS):
-        rows = pl.ds(g * G, G)
+    for g in range(PARTS):
+        rows = pl.ds(g * (ROWS // PARTS), ROWS // PARTS)
         staged[rows, :] = a_ref[rows, :] - dot(wcat_ref[rows, :], s)
         copy = pltpu.make_async_copy(staged.at[rows], o_ref.at[rows], sem.at[g])
         copy.start()
@@ -393,7 +397,7 @@
         out_shape=jax.ShapeDtypeStruct((ROWS, COLS), f32),
         in_specs=[pl.BlockSpec(memory_space=pltpu.VMEM)] * 3,
         out_specs=pl.BlockSpec(memory_space=pl.ANY),
-        scratch_shapes=[pltpu.VMEM((ROWS, COLS), f32), pltpu.SemaphoreType.DMA((GROUPS,))],
+        scratch_shapes=[pltpu.VMEM((ROWS, COLS), f32), pltpu.SemaphoreType.DMA((PARTS,))],
         compiler_params=pltpu.CompilerParams(vmem_limit_bytes=16 << 20),
         name="update",
     )(a, wcat, s)

time: 40.1 us -> 40 us (level)
  no operation moved by 1% of the time
where the time goes in v4:
time: 40 us; the launch traced here: 39.9 us
  Pallas kernels  39.9 us (100%)
    pallas_call x1, Pallas kernels, chain(): pl.pallas_call(chain_kernel, out_shape=[pltpu.VMEM((ROWS, COLS), f32), pl...  37.5 us
    pallas_call x1, Pallas kernels, update(): pl.pallas_call(update_kernel, out_shape=jax.ShapeDtypeStruct((ROWS, COLS)...  2.38 us

profile of v4, /device:TPU:1, one launch (start us, length us, event | category | flops | bytes accessed | tf_op | source)
XLA Modules:
  0.0 39.9 jit_solution(8737758977732370313)
XLA Ops:
  0.0 37.5 %chain.1 = (f32[2048,512]{1,0:T(8,128)S(1)}, bf16[2048,384]{1,0:T(8,128)(2,1)S(1)}, f32[128,512]{1,0:T(8,128)S(1)}) custom-call(f32[2048,512]{1,0:T(8,128)} %e_ref.1, f32[2048,128]{1,0:T(8,128)} %v0_ref.1, f32[2048,128]{1,0:T(8,128)} %w0_ref.1, f32[2048,128]{1,0:T(8,128)} %v1_ref.1, f32[2048,128]{1,0:T(8,128)} %w1_ref.1, f32[256,128]{1,0:T(8,128)} %y_ref.1, ...), custom_call_target="tpu_custom_call" | custom-call | tf_op jit(solution)/shard_map/chain/pallas_call | solution.py:329
  37.5 2.4 %update.1 = f32[2048,512]{1,0:T(8,128)} custom-call(f32[2048,512]{1,0:T(8,128)S(1)} %get-tuple-element.8.a_ref, bf16[2048,384]{1,0:T(8,128)(2,1)S(1)} %get-tuple-element.9.wcat_ref, f32[128,512]{1,0:T(8,128)S(1)} %get-tuple-element.10.s_ref), custom_call_target="tpu_custom_call" | custom-call | tf_op jit(solution)/shard_map/update/pallas_call | solution.py:395

commit v5 on v4

--- a/solution.py
+++ b/solution.py
@@ -224,8 +224,6 @@
     get_e[6].wait()
     first(5, 6)
     y_relay_far(1)
-    get_w.wait()
-    w_own()
     pl.semaphore_wait(know_b, 3)
     pl.semaphore_signal(know_c, inc=1, device_id=chip_at(1, 0), device_id_type=MESH)
     second(4, 5)
@@ -242,6 +240,8 @@
     total[...] = block(col) + block(other_col) + block(far_col)
     y_rest_own()
     total[...] += block(up_col) + block(down_col)
+    get_w.wait()
+    w_own()
 
     for side in (1, 0):
         edge, c, offset = edges[1 - side], (COL - 1) * (1 - side), (SHARD - B) * (1 - side)

time: 40 us -> 39.9 us (level)
  no operation moved by 1% of the time
where the time goes in v5:
time: 39.9 us; the launch traced here: 39.8 us
  Pallas kernels  39.8 us (100%)
    pallas_call x1, Pallas kernels, chain(): pl.pallas_call(chain_kernel, out_shape=[pltpu.VMEM((ROWS, COLS), f32), pl...  37.4 us
    pallas_call x1, Pallas kernels, update(): pl.pallas_call(update_kernel, out_shape=jax.ShapeDtypeStruct((ROWS, COLS)...  2.37 us

profile of v5, /device:TPU:1, one launch (start us, length us, event | category | flops | bytes accessed | tf_op | source)
XLA Modules:
  0.0 39.8 jit_solution(850425619879404846)
XLA Ops:
  0.0 37.4 %chain.1 = (f32[2048,512]{1,0:T(8,128)S(1)}, bf16[2048,384]{1,0:T(8,128)(2,1)S(1)}, f32[128,512]{1,0:T(8,128)S(1)}) custom-call(f32[2048,512]{1,0:T(8,128)} %e_ref.1, f32[2048,128]{1,0:T(8,128)} %v0_ref.1, f32[2048,128]{1,0:T(8,128)} %w0_ref.1, f32[2048,128]{1,0:T(8,128)} %v1_ref.1, f32[2048,128]{1,0:T(8,128)} %w1_ref.1, f32[256,128]{1,0:T(8,128)} %y_ref.1, ...), custom_call_target="tpu_custom_call" | custom-call | tf_op jit(solution)/shard_map/chain/pallas_call | solution.py:329
  37.4 2.4 %update.1 = f32[2048,512]{1,0:T(8,128)} custom-call(f32[2048,512]{1,0:T(8,128)S(1)} %get-tuple-element.8.a_ref, bf16[2048,384]{1,0:T(8,128)(2,1)S(1)} %get-tuple-element.9.wcat_ref, f32[128,512]{1,0:T(8,128)S(1)} %get-tuple-element.10.s_ref), custom_call_target="tpu_custom_call" | custom-call | tf_op jit(solution)/shard_map/update/pallas_call | solution.py:395
